TPU v7x, 32 devices: a whole 2x2x4 slice. The times are simulated.
32 devices in a mesh: grp: 2 (over y), ctx: 1, mdl: 8 (over z, x), dp: 2 (over core).
Axes of the slice: x: 2, y: 2, z: 4, core: 2. Of those that a mesh axis runs over, the one named last changes fastest.
Arguments:
- layer_input: bfloat16 [4, 1024, 2560], P(('grp', 'dp'), 'ctx', 'mdl'), parts along dimension 0, may hold values from -6 to 6
- read_weight: bfloat16 [2560, 128], P('mdl'), may hold values from -0.125 to 0.125
- head_inputs: bfloat16 [4, 1024, 5120], P(('grp', 'dp'), 'ctx', 'mdl'), parts along dimension 0, may hold values from -6 to 6
- write_vectors: bfloat16 [4, 1024, 128], P(('grp', 'dp'), 'ctx'), parts along dimension 0, may hold values from -0.0034179688 to 0.0034179688
- log_decay: float32 [4, 80, 1024], P(('grp', 'dp'), 'mdl', 'ctx'), parts along dimension 0, may hold values from -1 to 0
- segment_ids: int32 [4, 1024], P(('grp', 'dp'), 'ctx'), parts along dimension 0, may hold values from 0 to 3, never falling along the last dimension, each value on 1 to 512 neighbouring positions
- out_grad: bfloat16 [4, 1024, 5120], P(('grp', 'dp'), 'ctx', 'mdl'), parts along dimension 0, may hold values from -0.0029296875 to 0.0029296875
Outputs:
- head_outputs: bfloat16 [4, 1024, 5120], P(('grp', 'dp'), 'ctx', 'mdl'), parts along dimension 0
- read_grad: float32 [256, 2560], P(('grp', 'ctx', 'dp'), 'mdl'), parts along dimension 0
There are 2 independent parts, one for each index of `grp`. A program takes and returns all parts, laid end to end along the dimension named above; an argument that names none is the same for every part. Nothing has to cross between parts.
Inputs may be any that keep to these rules, and one draw needn't show every extreme that they name: `segment_ids`: segment numbers never fall along a trace; each segment is a run of at most 512 positions.
All inputs are finite; a program needn't handle non-finite values.
Results may differ from a plain program's by a relative error of at most 0.015.
Values may be sent and summed in bfloat16 or wider, within the bound.
A program may use at most 64 MiB of HBM per device.

v0:
```python
import jax
import jax.numpy as jnp
from jax import lax
from jax.sharding import PartitionSpec as P

BLOCK_LEN = 512


def shifted(value, axis, by):
    count = lax.axis_size(axis)
    pairs = [(i, i + by) for i in range(count) if 0 <= i + by < count]
    return lax.ppermute(value, axis, pairs)


def join_parts(earlier, later):
    early_first, early_last, early_pass, leading_state = earlier
    later_first, later_last, later_pass, later_state = later
    linked = jnp.logical_or(
        early_last == later_first, jnp.logical_or(early_last < 0.0, later_first < 0.0)
    )
    carried = later_pass * linked.astype(jnp.float32)[..., None]
    front_seg = jnp.where(early_first < 0.0, later_first, early_first)
    back_seg = jnp.where(later_last < 0.0, early_last, later_last)
    return (
        front_seg,
        back_seg,
        early_pass * carried,
        later_state + carried[..., None, None] * leading_state,
    )


def per_device(
    layer_input, read_weight, head_inputs, write_vectors, log_decay, segment_ids, out_grad
):
    trace_count, length, model_cols = layer_input.shape
    head_count = log_decay.shape[1]
    head_dim = head_inputs.shape[2] // head_count
    state_dim = write_vectors.shape[2]
    block_count = length // BLOCK_LEN
    rows_all = trace_count * length
    flat_count = trace_count * block_count
    flat_input = layer_input.reshape(rows_all, model_cols)
    partial_value = jnp.dot(flat_input, read_weight, preferred_element_type=jnp.float32)
    readout = lax.psum(partial_value.astype(jnp.bfloat16), "mdl")
    segments = segment_ids.astype(jnp.float32).reshape(trace_count, block_count, BLOCK_LEN)
    decays = log_decay.reshape(trace_count, head_count, block_count, BLOCK_LEN)
    positions = jnp.arange(BLOCK_LEN)
    cumulative = jnp.cumsum(decays, axis=3)
    closing = cumulative[..., -1:]
    at_end = (segments == segments[..., -1:]).astype(jnp.float32)
    end_weight = jnp.exp(closing - cumulative) * at_end[:, None]
    values = head_inputs.reshape(trace_count, block_count, BLOCK_LEN, head_count, head_dim)
    keys_block = write_vectors.reshape(trace_count, block_count, BLOCK_LEN, state_dim)
    weighted = (values * jnp.transpose(end_weight, (0, 2, 3, 1))[..., None]).astype(jnp.bfloat16)
    block_states = jnp.einsum(
        "bkqhp,bkqn->kbhpn", weighted, keys_block, preferred_element_type=jnp.float32
    )
    front_seg = jnp.transpose(segments[..., 0])
    back_seg = jnp.transpose(segments[..., -1])
    single = (front_seg == back_seg).astype(jnp.float32)
    through = jnp.exp(jnp.transpose(closing[..., 0], (2, 0, 1))) * single[..., None]
    neutral = (
        -jnp.ones((trace_count,), jnp.float32),
        -jnp.ones((trace_count,), jnp.float32),
        jnp.ones((trace_count, head_count), jnp.float32),
        jnp.zeros((trace_count, head_count, head_dim, state_dim), jnp.float32),
    )

    def absorb(running, pieces):
        return (join_parts(running, pieces), running)

    device_total, prefixes = lax.scan(absorb, neutral, (front_seg, back_seg, through, block_states))
    position = lax.axis_index("ctx")

    def relay_once(iteration, incoming):
        outgoing = join_parts(incoming, device_total)
        shifted_lines = shifted((outgoing[0], outgoing[1], outgoing[2], outgoing[3]), "ctx", 1)
        return tuple(
            (
                jnp.where(position == 0, anchor, arrived)
                for anchor, arrived in zip(neutral, shifted_lines)
            )
        )

    entering = lax.fori_loop(0, lax.axis_size("ctx") - 1, relay_once, neutral)
    starts = join_parts(entering, prefixes)
    start_low = starts[3].astype(jnp.bfloat16)
    prior_seg = jnp.transpose(starts[1])
    coupled_items = (segments == prior_seg[..., None]).astype(jnp.float32)
    entry_gain = jnp.exp(cumulative) * coupled_items[:, None]
    gain_rows = jnp.transpose(entry_gain, (0, 2, 3, 1))[..., None]
    readout_block = readout.reshape(trace_count, block_count, BLOCK_LEN, state_dim)
    grads_block = out_grad.reshape(trace_count, block_count, BLOCK_LEN, head_count, head_dim)
    carried_out = (
        jnp.einsum(
            "bkqn,kbhpn->bkqhp", readout_block, start_low, preferred_element_type=jnp.float32
        )
        * gain_rows
    )
    per_head = jnp.einsum(
        "bkqhp,kbhpn->bkqhn", grads_block, start_low, preferred_element_type=jnp.float32
    )
    carried_back = jnp.sum(per_head * gain_rows, axis=3)
    causal = positions[:, None] >= positions[None, :]

    def inside(pieces):
        read_rows, key_rows, value_rows, grad_rows, cum_rows, seg_rows = pieces
        allowed = jnp.logical_and(causal, seg_rows[:, None] == seg_rows[None, :])
        spread = cum_rows[:, :, None] - cum_rows[:, None, :]
        weight = jnp.where(allowed[None], jnp.exp(jnp.where(allowed[None], spread, 0.0)), 0.0)
        scores = jnp.einsum("tn,sn->ts", read_rows, key_rows, preferred_element_type=jnp.float32)
        blend_factor = (weight * scores[None]).astype(jnp.bfloat16)
        inside_out = jnp.einsum(
            "hts,shp->thp", blend_factor, value_rows, preferred_element_type=jnp.float32
        )
        products = jnp.einsum(
            "thp,shp->hts", grad_rows, value_rows, preferred_element_type=jnp.float32
        )
        response = jnp.sum(weight * products, axis=0).astype(jnp.bfloat16)
        inside_back = jnp.dot(response, key_rows, preferred_element_type=jnp.float32)
        return (inside_out, inside_back)

    own_out, own_back = lax.map(
        inside,
        (
            readout_block.reshape(flat_count, BLOCK_LEN, state_dim),
            keys_block.reshape(flat_count, BLOCK_LEN, state_dim),
            values.reshape(flat_count, BLOCK_LEN, head_count, head_dim),
            grads_block.reshape(flat_count, BLOCK_LEN, head_count, head_dim),
            jnp.transpose(cumulative, (0, 2, 1, 3)).reshape(flat_count, head_count, BLOCK_LEN),
            segments.reshape(flat_count, BLOCK_LEN),
        ),
    )
    total_out = (
        own_out.reshape(trace_count, block_count, BLOCK_LEN, head_count, head_dim) + carried_out
    )
    head_outputs = total_out.astype(jnp.bfloat16).reshape(
        trace_count, length, head_count * head_dim
    )
    back_part = (
        own_back.reshape(trace_count, block_count, BLOCK_LEN, state_dim) + carried_back
    ).reshape(rows_all, state_dim)
    read_back = lax.psum(back_part.astype(jnp.bfloat16), "mdl")
    read_grad = lax.psum_scatter(
        lax.dot_general(
            read_back, flat_input, (((0,), (0,)), ((), ())), preferred_element_type=jnp.float32
        ),
        ("ctx", "dp"),
        scatter_dimension=0,
        tiled=True,
    )
    return (head_outputs, read_grad)


def solution(mesh):
    placed = (
        P(("grp", "dp"), "ctx", "mdl"),
        P("mdl", None),
        P(("grp", "dp"), "ctx", "mdl"),
        P(("grp", "dp"), "ctx", None),
        P(("grp", "dp"), "mdl", "ctx"),
        P(("grp", "dp"), "ctx"),
        P(("grp", "dp"), "ctx", "mdl"),
    )
    return jax.shard_map(
        per_device,
        mesh=mesh,
        in_specs=placed,
        out_specs=(P(("grp", "dp"), "ctx", "mdl"), P(("grp", "ctx", "dp"), "mdl")),
        check_vma=False,
    )
```

profile of v0, /device:TPU:0, one launch (start us, length us, event | category | flops | bytes accessed | tf_op | source)
XLA Modules:
  0.0 198.6 jit_solution(15188353820331368359)
XLA Ops:
  7.2 0.0 all-reduce.3.cloned.1.call-start
  7.2 1.0 copy-done
  8.3 2.0 %convolution_convert_fusion = bf16[1024,128]{1,0:T(8,128)(2,1)} fusion(bf16[320,128]{1,0:T(8,128)(2,1)} %param.12, bf16[1,1024,320]{1,2,0:T(8,128)(2,1)S(1)} %copy-done), kind=kOutput, calls=%fused_computation.50 | convolution fusion | flops 84017152 | bytes 999424 | tf_op jit(solution)/shard_map/dot_general | solution.py:43
  10.3 0.0 all-reduce.5.cloned.1.call-start
  10.3 0.8 copy.90
  11.1 2.3 %reduce-window.6 = f32[1,10,2,4,128]{4,1,2,3,0:T(8,128)S(1)} reduce-window(f32[1,10,2,4,128]{4,1,2,3,0:T(8,128)S(1)} %copy.90, f32[]{:T(128)} %constant.61.clone.1), window={size=1x1x1x1x128 pad=0_0x0_0x0_0x0_0x127_0}, to_apply=%region_1.0 | reduce-window | flops 1300480 | bytes 81924 | tf_op jit(solution)/shard_map/reduce-window
  13.4 0.1 slice.21
  13.5 0.7 convert_element_type.66
  14.2 0.7 convert_reduce_fusion
  15.0 0.3 copy.94
  15.3 0.1 copy.92
  15.4 0.2 bitcast_add_fusion.1
  15.6 0.1 fusion.44
  15.7 0.1 copy.120
  15.8 0.1 compare_convert_fusion.1
  15.9 0.1 copy.102
  16.1 0.7 multiply_bitcast_fusion.1
  16.8 0.2 copy.103
  17.0 2.4 %copy.89 = bf16[1,1024,640]{1,2,0:T(8,128)(2,1)} copy(bf16[1,1024,640]{2,1,0:T(8,128)(2,1)} %param.13) | data formatting | bytes 2621440 | tf_op args[2]
  19.4 3.6 %reshape_reshape.15 = bf16[2,512,10,64]{1,0,3,2:T(2,128)(2,1)S(1)} reshape(bf16[1,1024,640]{1,2,0:T(8,128)(2,1)} %copy.89) | data formatting | bytes 2621440 | tf_op jit(solution)/shard_map/reshape;reshape | solution.py:128
  23.0 1.3 copy.97
  24.3 2.3 %multiply_convert_fusion.6 = bf16[2,512,10,64]{1,0,3,2:T(2,128)(2,1)} fusion(bf16[2,512,10,64]{1,0,3,2:T(2,128)(2,1)S(1)} %reshape_reshape.15, f32[2,512,10]{1,0,2:T(2,128)S(1)} %copy.103), kind=kLoop, calls=%fused_computation.46 | loop fusion | flops 1966080 | bytes 2662400 | tf_op jit(solution)/shard_map/convert_element_type | solution.py:54
  26.6 0.1 copy.121
  26.7 0.1 bitcast_multiply_fusion.2
  26.7 1.8 fusion.32
  28.6 8.4 %while.40 = (s32[]{:T(128)}, f32[1]{0:T(128)}, f32[1,10]{1,0:T(1,128)S(1)}, f32[1,10,64,128]{3,2,1,0:T(8,128)S(1)}, f32[2,1]{0,1:T(1,128)S(1)}, /*index=5*/f32[2...) while((s32[]{:T(128)}, f32[1]{0:T(128)}, ...), condition=%wide.region_7.8_spmd.clone.clone, body=%wide.region_6.7_spmd.clone.sunk.clone | while | flops 327741 | bytes 1640430 | solution.py:72
  28.6 0.6 constant_dynamic-slice_fusion.9
  30.5 0.8 bitcast_dynamic-update-slice_fusion.3
  31.3 0.1 bitcast_add_fusion.4
  32.7 0.6 constant_dynamic-slice_fusion.9
  34.7 0.8 bitcast_dynamic-update-slice_fusion.3
  35.4 0.1 bitcast_add_fusion.4
  36.8 0.1 dynamic_update_slice.47
  36.9 0.1 compare_convert_fusion
  37.0 0.2 copy.107
  37.2 0.7 multiply_bitcast_fusion
  37.9 0.2 copy.108
  38.1 2.5 %copy.96 = bf16[1,1024,640]{1,2,0:T(8,128)(2,1)} copy(bf16[1,1024,640]{2,1,0:T(8,128)(2,1)} %param.17) | data formatting | bytes 2621440 | tf_op args[6]
  40.6 3.6 %reshape_reshape.19 = bf16[2,512,10,64]{1,0,3,2:T(2,128)(2,1)S(1)} reshape(bf16[1,1024,640]{1,2,0:T(8,128)(2,1)} %copy.96) | data formatting | bytes 2621440 | tf_op jit(solution)/shard_map/reshape;reshape | solution.py:129
  44.2 0.2 copy.98
  44.4 1.4 copy.99
  45.7 3.0 %fusion.29 = f32[2,512,128]{1,2,0:T(8,128)} fusion(f32[2,512,10]{1,2,0:T(8,128)S(1)} %copy.108, f32[2,1,10,64,128]{4,3,2,1,0:T(8,128)} %get-tuple-element.146, f32[2,10]{1,0:T(2,128)S(1)} %bitcast.194, bf16[2,512,10,64]{1,0,3,2:T(2,128)(2,1)S(1)} %reshape_reshape.19), kind=kOutput, calls=%fused_computation.44 | convolution fusion | flops 170590208 | bytes 2531408 | tf_op jit(solution)/shard_map/bkqhp,kbhpn->bkqhn/dot_general | solution.py:100
  48.7 35.9 %all-reduce.3.cloned.1.call-done = bf16[2,512,128]{2,1,0:T(8,128)(2,1)} async-done(((bf16[2,512,128]{2,1,0:T(8,128)(2,1)}), bf16[2,512,128]{2,1,0:T(8,128)(2,1)}) %all-reduce.3.cloned.1.call-update) | async-done | bytes 262160 | tf_op jit(solution)/shard_map/psum | solution.py:44
  84.7 23.7 %while.39 = (s32[]{:T(128)}, f32[2,512,10,64]{1,3,2,0:T(8,128)}, f32[2,512,128]{1,2,0:T(8,128)}, bf16[2,512,10,64]{1,3,2,0:T(8,128)(2,1)}, f32[2,512]{1,0:T(2,12...) while((s32[]{:T(128)}, f32[2,512,10,64]{1,3,2,0:T(8,128)}, ...), condition=%wide.region_5.6_spmd.clone.clone, body=%wide.region_3.5_spmd.clone.sunk.clone | while | flops 832045056 | bytes 18532508 | solution.py:123
  84.7 1.2 fusion.80
  85.9 0.2 fusion.81
  86.1 5.5 %fusion.82 = f32[2,512,10,64]{1,3,2,0:T(8,128)} fusion(f32[2,512,10,64]{1,3,2,0:T(8,128)} %get-tuple-element.535, s32[]{:T(128)} %get-tuple-element.534, f32[512,512]{1,0:T(8,128)S(1)} %fusion.80, f32[10,512]{1,0:T(8,128)S(1)} %dynamic-slice_bitcast_fusion.3, pred[512,512]{1,0:T(8,128)(4,1)S(1)} %fusion.81, ...), kind=kOutput, calls=%fused_computation.7.clone.1.clone | convolution fusion | flops 348651520 | bytes 3343360 | tf_op jit(solution)/shard_map/while/body/eval_jaxpr/hts,shp->thp/dot_general | solution.py:113
  91.7 3.8 %multiply_reduce_fusion.3 = bf16[512,512]{1,0:T(8,128)(2,1)S(1)} fusion(f32[10,512]{1,0:T(8,128)S(1)} %dynamic-slice_bitcast_fusion.3, pred[512,512]{1,0:T(8,128)(4,1)S(1)} %fusion.81, bf16[2,512,10,64]{1,3,2,0:T(8,128)(2,1)S(1)} %copy-done.5, s32[]{:T(128)} %get-tuple-element.534, bf16[2,512,10,64]{1,3,2,0:T(8,128)(2,1)S(1)} %copy-done.4), kind=kOutput, calls=%fused_computation.1.clone.1.clone | convolution fusion | flops 348389376 | bytes 2163712 | tf_op jit(solution)/shard_map/while/body/eval_jaxpr/thp,shp->hts/dot_general | solution.py:116
  95.5 1.0 fusion.83
  96.5 1.2 fusion.80
  97.7 0.2 fusion.81
  98.0 5.5 %fusion.82 = f32[2,512,10,64]{1,3,2,0:T(8,128)} fusion(f32[2,512,10,64]{1,3,2,0:T(8,128)} %get-tuple-element.535, s32[]{:T(128)} %get-tuple-element.534, f32[512,512]{1,0:T(8,128)S(1)} %fusion.80, f32[10,512]{1,0:T(8,128)S(1)} %dynamic-slice_bitcast_fusion.3, pred[512,512]{1,0:T(8,128)(4,1)S(1)} %fusion.81, ...), kind=kOutput, calls=%fused_computation.7.clone.1.clone | convolution fusion | flops 348651520 | bytes 3343360 | tf_op jit(solution)/shard_map/while/body/eval_jaxpr/hts,shp->thp/dot_general | solution.py:113
  103.5 3.8 %multiply_reduce_fusion.3 = bf16[512,512]{1,0:T(8,128)(2,1)S(1)} fusion(f32[10,512]{1,0:T(8,128)S(1)} %dynamic-slice_bitcast_fusion.3, pred[512,512]{1,0:T(8,128)(4,1)S(1)} %fusion.81, bf16[2,512,10,64]{1,3,2,0:T(8,128)(2,1)S(1)} %copy-done.5, s32[]{:T(128)} %get-tuple-element.534, bf16[2,512,10,64]{1,3,2,0:T(8,128)(2,1)S(1)} %copy-done.4), kind=kOutput, calls=%fused_computation.1.clone.1.clone | convolution fusion | flops 348389376 | bytes 2163712 | tf_op jit(solution)/shard_map/while/body/eval_jaxpr/thp,shp->hts/dot_general | solution.py:116
  107.4 1.0 fusion.83
  108.4 2.1 %add_convert_fusion.2 = bf16[2,512,128]{1,2,0:T(8,128)(2,1)} fusion(f32[2,512,128]{1,2,0:T(8,128)} %get-tuple-element.149, f32[2,512,128]{1,2,0:T(8,128)} %fusion.29), kind=kLoop, calls=%fused_computation.56 | loop fusion | flops 262144 | bytes 1310720 | tf_op jit(solution)/shard_map/convert_element_type | solution.py:143
  110.5 1.8 copy.113
  112.4 0.0 reduce-scatter.2.cloned.1.call-start
  112.4 70.0 %all-reduce.5.cloned.1.call-done = bf16[1024,128]{1,0:T(8,128)(2,1)} async-done(((bf16[1024,128]{1,0:T(8,128)(2,1)}), bf16[1024,128]{1,0:T(8,128)(2,1)}) %all-reduce.5.cloned.1.call-update) | async-done | bytes 262160 | tf_op jit(solution)/shard_map/psum | solution.py:143
  182.4 2.0 %fusion.35 = f32[128,320]{1,0:T(8,128)} fusion(bf16[1024,128]{1,0:T(8,128)(2,1)} %all-reduce.5.cloned.1.call-done, bf16[1,1024,320]{1,2,0:T(8,128)(2,1)S(1)} %copy-done), kind=kOutput, calls=%fused_computation.51 | convolution fusion | flops 83886080 | bytes 1081344 | tf_op jit(solution)/shard_map/dot_general | solution.py:145
  184.4 1.6 add_convert_fusion
  186.1 1.4 copy.109
  187.4 1.0 reshape.298
  188.4 1.4 copy.114
  189.8 2.3 %reduce-scatter.2.cloned.1.call-done = f32[64,320]{1,0:T(8,128)} async-done(((f32[128,320]{1,0:T(8,128)}), f32[64,320]{1,0:T(8,128)}) %reduce-scatter.2.cloned.1.call-update) | async-done | bytes 81936 | tf_op jit(solution)/shard_map/reduce_scatter | solution.py:144
  (48 shorter events, 0.4 us)
Async XLA Ops:
  7.2 1.1 copy-start
  7.2 77.5 %all-reduce.3.cloned.1.call-start = ((), (), s32[]{:S(2)}) async-start(), calls=%async_computation.1 | async-start | bytes 524288 | tf_op jit(solution)/shard_map/psum | solution.py:44
  10.3 172.1 %all-reduce.5.cloned.1.call-start = ((), (), s32[]{:S(2)}) async-start(), calls=%async_computation.2 | async-start | bytes 524288 | tf_op jit(solution)/shard_map/psum | solution.py:143
  23.0 3.8 %copy-start.1 = (bf16[1,1024,128]{2,1,0:T(8,128)(2,1)S(1)}, bf16[1,1024,128]{2,1,0:T(8,128)(2,1)}, u32[]{:S(2)}) copy-start(bf16[1,1024,128]{2,1,0:T(8,128)(2,1)} %param.14) | copy-start | bytes 786436
  38.1 7.6 %copy-start.6 = (f32[2,512,10]{1,2,0:T(8,128)}, f32[2,512,10]{1,2,0:T(8,128)S(1)}, u32[]{:S(2)}) copy-start(f32[2,512,10]{1,2,0:T(8,128)S(1)} %copy.108) | copy-start | bytes 122884
  86.1 5.5 %copy-start.4 = (bf16[2,512,10,64]{1,3,2,0:T(8,128)(2,1)S(1)}, bf16[2,512,10,64]{1,3,2,0:T(8,128)(2,1)}, u32[]{:S(2)}) copy-start(bf16[2,512,10,64]{1,3,2,0:T(8,128)(2,1)} %get-tuple-element.546) | copy-start | bytes 3932164 | tf_op jit(solution)/shard_map/while
  86.1 5.5 %copy-start.5 = (bf16[2,512,10,64]{1,3,2,0:T(8,128)(2,1)S(1)}, bf16[2,512,10,64]{1,3,2,0:T(8,128)(2,1)}, u32[]{:S(2)}) copy-start(bf16[2,512,10,64]{1,3,2,0:T(8,128)(2,1)} %get-tuple-element.551) | copy-start | bytes 3932164 | tf_op jit(solution)/shard_map/while
  98.0 5.6 %copy-start.4 = (bf16[2,512,10,64]{1,3,2,0:T(8,128)(2,1)S(1)}, bf16[2,512,10,64]{1,3,2,0:T(8,128)(2,1)}, u32[]{:S(2)}) copy-start(bf16[2,512,10,64]{1,3,2,0:T(8,128)(2,1)} %get-tuple-element.546) | copy-start | bytes 3932164 | tf_op jit(solution)/shard_map/while
  98.0 5.5 %copy-start.5 = (bf16[2,512,10,64]{1,3,2,0:T(8,128)(2,1)S(1)}, bf16[2,512,10,64]{1,3,2,0:T(8,128)(2,1)}, u32[]{:S(2)}) copy-start(bf16[2,512,10,64]{1,3,2,0:T(8,128)(2,1)} %get-tuple-element.551) | copy-start | bytes 3932164 | tf_op jit(solution)/shard_map/while
  108.4 76.0 %copy-start.2 = (bf16[2,512,128]{2,1,0:T(8,128)(2,1)S(1)}, bf16[2,512,128]{2,1,0:T(8,128)(2,1)}, u32[]{:S(2)}) copy-start(bf16[2,512,128]{2,1,0:T(8,128)(2,1)} %get-tuple-element.592) | copy-start | bytes 786436
  108.4 76.0 %copy-start.3 = (f32[2,512,10,64]{1,3,2,0:T(8,128)S(1)}, f32[2,512,10,64]{1,3,2,0:T(8,128)}, u32[]{:S(2)}) copy-start(f32[2,512,10,64]{1,3,2,0:T(8,128)} %get-tuple-element.145) | copy-start | bytes 7864324
  112.4 79.7 %reduce-scatter.2.cloned.1.call-start = ((), (), s32[]{:S(2)}) async-start(), calls=%async_computation.3 | async-start | bytes 294912 | tf_op jit(solution)/shard_map/reduce_scatter | solution.py:144
Sparse Core Ops, SparseCore 0:
  11.4 73.2 all-reduce.2
  112.5 69.8 all-reduce.4
  185.2 6.8 reduce-scatter.1
where the time goes:
time: 199 us
  waiting for transfers between devices  108 us (54%)
  matrix products  33.6 us (17%)
  local copies, waits for them, and re-layouts  25.3 us (13%)
  between operations  14 us (7%)
  other arithmetic  12.1 us (6%)
  loops' own time  5.3 us (3%)
    psum x1, waiting for transfers between devices, per_device(): read_back = lax.psum(back_part.astype(jnp.bfloat16), 'mdl')  70 us
    psum x1, waiting for transfers between devices, per_device(): readout = lax.psum(partial_value.astype(jnp.bfloat16), 'mdl')  35.9 us
    dot_general x2, matrix products, inside(): jnp.einsum('hts,shp->thp', blend_factor, value_rows, preferred_element_ty...  11.1 us
    unnamed x19, local copies, waits for them, and re-layouts  10.5 us
    dot_general x2, matrix products, inside(): jnp.einsum('thp,shp->hts', grad_rows, value_rows, preferred_element_type=...  7.62 us
    another operation x1, loops' own time, per_device(): lax.scan(absorb, neutral, (front_seg, back_seg, through, block_states))  5.19 us
  transfers between devices with their start and end apart: 3, of which 3 were waited for; matrix products, arithmetic and copies ran while one was open for 19% of the time, Pallas kernels for 0%

commit v1 on v0

--- a/solution.py
+++ b/solution.py
@@ -41,7 +41,9 @@
     flat_count = trace_count * block_count
     flat_input = layer_input.reshape(rows_all, model_cols)
     partial_value = jnp.dot(flat_input, read_weight, preferred_element_type=jnp.float32)
-    readout = lax.psum(partial_value.astype(jnp.bfloat16), "mdl")
+    x = partial_value.astype(jnp.bfloat16)
+    parts = lax.all_gather(x, "mdl")
+    readout = jnp.sum(parts, axis=0)
     segments = segment_ids.astype(jnp.float32).reshape(trace_count, block_count, BLOCK_LEN)
     decays = log_decay.reshape(trace_count, head_count, block_count, BLOCK_LEN)
     positions = jnp.arange(BLOCK_LEN)

time: 199 us -> 175 us (0.88)
  waiting for transfers between devices: 108 us -> 84.8 us
  matrix products: 33.6 us -> 31.1 us
    psum x1 -> x0, waiting for transfers between devices: 35.9 us -> none  [per_device(): readout = lax.psum(partial_value.astype(jnp.bfloat16), 'mdl')]
    all_gather x0 -> x1, waiting for transfers between devices: none -> 13.9 us  [per_device(): parts = lax.all_gather(x, 'mdl')]
    unnamed x19 -> x15, local copies, waits for them, and re-layouts: 10.5 us -> 10.5 us
  transfers between devices with their start and end apart: 3 -> 3, of which waited for: 3 -> 3; matrix products, arithmetic and copies ran while one was open for 19% -> 22% of each run, Pallas kernels for 0% -> 0%
where the time goes in v1:
time: 175 us
  waiting for transfers between devices  84.8 us (48%)
  matrix products  31.1 us (18%)
  local copies, waits for them, and re-layouts  26 us (15%)
  between operations  13.9 us (8%)
  other arithmetic  13.4 us (8%)
  loops' own time  5.15 us (3%)
    psum x1, waiting for transfers between devices, per_device(): read_back = lax.psum(back_part.astype(jnp.bfloat16), 'mdl')  69.2 us
    all_gather x1, waiting for transfers between devices, per_device(): parts = lax.all_gather(x, 'mdl')  13.9 us
    dot_general x2, matrix products, inside(): jnp.einsum('hts,shp->thp', blend_factor, value_rows, preferred_element_ty...  11.1 us
    unnamed x15, local copies, waits for them, and re-layouts  10.5 us
    dot_general x2, matrix products, inside(): jnp.einsum('thp,shp->hts', grad_rows, value_rows, preferred_element_type=...  7.69 us
    another operation x1, loops' own time, per_device(): lax.scan(absorb, neutral, (front_seg, back_seg, through, block_states))  4.79 us
    another operation x1, local copies, waits for them, and re-layouts, per_device(): values.reshape(flat_count, BLOCK_LEN, head_count, head_dim)  3.57 us
    another operation x1, local copies, waits for them, and re-layouts, per_device(): grads_block.reshape(flat_count, BLOCK_LEN, head_count, head_dim)  3.55 us
  transfers between devices with their start and end apart: 3, of which 3 were waited for; matrix products, arithmetic and copies ran while one was open for 22% of the time, Pallas kernels for 0%

profile of v1, /device:TPU:0, one launch (start us, length us, event | category | flops | bytes accessed | tf_op | source)
XLA Modules:
  0.0 174.5 jit_solution(10171443254349821394)
XLA Ops:
  7.2 1.0 copy-done
  8.3 2.0 %convolution_convert_fusion = bf16[1024,128]{1,0:T(8,128)(2,1)} fusion(bf16[320,128]{1,0:T(8,128)(2,1)} %param.12, bf16[1,1024,320]{1,2,0:T(8,128)(2,1)S(1)} %copy-done), kind=kOutput, calls=%fused_computation.50 | convolution fusion | flops 84017152 | bytes 999424 | tf_op jit(solution)/shard_map/dot_general | solution.py:43
  10.3 0.8 copy.90
  11.1 2.3 %reduce-window.6 = f32[1,10,2,4,128]{4,1,2,3,0:T(8,128)S(1)} reduce-window(f32[1,10,2,4,128]{4,1,2,3,0:T(8,128)S(1)} %copy.90, f32[]{:T(128)} %constant.62.clone.1), window={size=1x1x1x1x128 pad=0_0x0_0x0_0x0_0x127_0}, to_apply=%region_1.0 | reduce-window | flops 1300480 | bytes 81924 | tf_op jit(solution)/shard_map/reduce-window
  13.4 0.1 slice.21
  13.5 0.7 convert_element_type.68
  14.2 0.7 convert_reduce_fusion
  15.0 0.3 copy.94
  15.3 0.1 copy.92
  15.4 0.2 bitcast_add_fusion.1
  15.6 0.1 fusion.43
  15.7 0.1 copy.120
  15.8 0.1 compare_convert_fusion.1
  15.9 0.2 copy.102
  16.1 0.7 multiply_bitcast_fusion.1
  16.8 0.2 copy.103
  17.0 2.4 %copy.89 = bf16[1,1024,640]{1,2,0:T(8,128)(2,1)} copy(bf16[1,1024,640]{2,1,0:T(8,128)(2,1)} %param.13) | data formatting | bytes 2621440 | tf_op args[2]
  19.4 3.6 %reshape_reshape.15 = bf16[2,512,10,64]{1,0,3,2:T(2,128)(2,1)S(1)} reshape(bf16[1,1024,640]{1,2,0:T(8,128)(2,1)} %copy.89) | data formatting | bytes 2621440 | tf_op jit(solution)/shard_map/reshape;reshape | solution.py:130
  23.0 1.3 copy.97
  24.3 2.3 %multiply_convert_fusion.6 = bf16[2,512,10,64]{1,0,3,2:T(2,128)(2,1)} fusion(bf16[2,512,10,64]{1,0,3,2:T(2,128)(2,1)S(1)} %reshape_reshape.15, f32[2,512,10]{1,0,2:T(2,128)S(1)} %copy.103), kind=kLoop, calls=%fused_computation.46 | loop fusion | flops 1966080 | bytes 2662400 | tf_op jit(solution)/shard_map/convert_element_type | solution.py:56
  26.6 0.1 copy.121
  26.7 1.8 %fusion.32 = f32[2,1,10,64,128]{4,3,2,1,0:T(8,128)S(1)} fusion(bf16[2,512,128,1]{2,1,3,0:T(8,128)(2,1)S(1)} %bitcast.182, bf16[2,512,10,64]{1,0,3,2:T(2,128)(2,1)} %multiply_convert_fusion.6), kind=kOutput, calls=%fused_computation.49 | convolution fusion | flops 167772160 | bytes 2228224 | tf_op jit(solution)/shard_map/bkqhp,bkqn->kbhpn/dot_general | solution.py:57
  28.5 0.1 bitcast_multiply_fusion.2
  28.6 8.1 %while.40 = (s32[]{:T(128)}, f32[1]{0:T(128)}, f32[1,10]{1,0:T(1,128)S(1)}, f32[1,10,64,128]{3,2,1,0:T(8,128)S(1)}, f32[2,1]{0,1:T(1,128)S(1)}, /*index=5*/f32[2...) while((s32[]{:T(128)}, f32[1]{0:T(128)}, ...), condition=%wide.region_7.8_spmd.clone.clone, body=%wide.region_6.7_spmd.clone.sunk.clone | while | flops 327741 | bytes 1640430 | solution.py:74
  28.6 0.7 constant_dynamic-slice_fusion.9
  30.5 0.8 bitcast_dynamic-update-slice_fusion.3
  31.3 0.1 bitcast_add_fusion.4
  32.6 0.7 constant_dynamic-slice_fusion.9
  34.5 0.8 bitcast_dynamic-update-slice_fusion.3
  35.3 0.1 bitcast_add_fusion.4
  36.5 0.1 dynamic_update_slice.47
  36.7 0.1 compare_convert_fusion
  36.7 0.2 copy.107
  36.9 0.7 multiply_bitcast_fusion
  37.6 0.2 copy.108
  37.8 2.5 %copy.96 = bf16[1,1024,640]{1,2,0:T(8,128)(2,1)} copy(bf16[1,1024,640]{2,1,0:T(8,128)(2,1)} %param.17) | data formatting | bytes 2621440 | tf_op args[6]
  40.3 3.6 %reshape_reshape.19 = bf16[2,512,10,64]{1,0,3,2:T(2,128)(2,1)S(1)} reshape(bf16[1,1024,640]{1,2,0:T(8,128)(2,1)} %copy.96) | data formatting | bytes 2621440 | tf_op jit(solution)/shard_map/reshape;reshape | solution.py:131
  43.9 0.2 copy.98
  44.1 1.4 copy.99
  45.5 3.0 %fusion.29 = f32[2,512,128]{1,2,0:T(8,128)} fusion(f32[2,512,10]{1,2,0:T(8,128)S(1)} %copy.108, f32[2,1,10,64,128]{4,3,2,1,0:T(8,128)} %get-tuple-element.146, f32[2,10]{1,0:T(2,128)S(1)} %bitcast.197, bf16[2,512,10,64]{1,0,3,2:T(2,128)(2,1)S(1)} %reshape_reshape.19), kind=kOutput, calls=%fused_computation.44 | convolution fusion | flops 170590208 | bytes 2531408 | tf_op jit(solution)/shard_map/bkqhp,kbhpn->bkqhn/dot_general | solution.py:102
  48.5 13.9 %all-gather.3.cloned.1.call-done = bf16[8192,128]{1,0:T(8,128)(2,1)} async-done(((bf16[1024,128]{1,0:T(8,128)(2,1)}), bf16[8192,128]{1,0:T(8,128)(2,1)}) %all-gather.3.cloned.1.call-update) | async-done | bytes 2097168 | tf_op jit(solution)/shard_map/all_gather | solution.py:45
  62.4 2.0 %reduce_sum.30 = bf16[1024,128]{1,0:T(8,128)(2,1)S(1)} reduce(bf16[8,1024,128]{2,1,0:T(8,128)(2,1)} %bitcast.186, bf16[]{:T(256)} %constant.63.clone.1), dimensions={0}, to_apply=%region_0.0 | reduce | flops 917504 | bytes 2359298 | tf_op jit(solution)/shard_map/reduce_sum | solution.py:46
  64.4 22.4 %while.39 = (s32[]{:T(128)}, f32[2,512,10,64]{1,3,2,0:T(8,128)}, f32[2,512,128]{1,2,0:T(8,128)}, bf16[2,512,10,64]{1,3,2,0:T(8,128)(2,1)}, f32[2,512]{1,0:T(2,12...) while((s32[]{:T(128)}, f32[2,512,10,64]{1,3,2,0:T(8,128)}, ...), condition=%wide.region_5.6_spmd.clone.clone, body=%wide.region_3.5_spmd.clone.sunk.clone | while | flops 832045056 | bytes 22726868 | solution.py:125
  64.6 0.3 fusion.80
  64.9 0.2 fusion.81
  65.2 5.5 %fusion.82 = f32[2,512,10,64]{1,3,2,0:T(8,128)} fusion(f32[2,512,10,64]{1,3,2,0:T(8,128)} %get-tuple-element.535, s32[]{:T(128)} %get-tuple-element.534, f32[512,512]{1,0:T(8,128)S(1)} %fusion.80, f32[10,512]{1,0:T(8,128)S(1)} %dynamic-slice_bitcast_fusion.3, pred[512,512]{1,0:T(8,128)(4,1)S(1)} %fusion.81, ...), kind=kOutput, calls=%fused_computation.7.clone.1.clone | convolution fusion | flops 348651520 | bytes 3343360 | tf_op jit(solution)/shard_map/while/body/eval_jaxpr/hts,shp->thp/dot_general | solution.py:115
  70.7 3.8 %multiply_reduce_fusion.3 = bf16[512,512]{1,0:T(8,128)(2,1)S(1)} fusion(f32[10,512]{1,0:T(8,128)S(1)} %dynamic-slice_bitcast_fusion.3, pred[512,512]{1,0:T(8,128)(4,1)S(1)} %fusion.81, bf16[2,512,10,64]{1,3,2,0:T(8,128)(2,1)S(1)} %copy-done.3, s32[]{:T(128)} %get-tuple-element.534, bf16[2,512,10,64]{1,3,2,0:T(8,128)(2,1)S(1)} %copy-done.2), kind=kOutput, calls=%fused_computation.1.clone.1.clone | convolution fusion | flops 348389376 | bytes 2163712 | tf_op jit(solution)/shard_map/while/body/eval_jaxpr/thp,shp->hts/dot_general | solution.py:118
  74.6 0.3 fusion.83
  74.9 0.8 copy-done.6
  75.7 0.3 fusion.80
  76.0 0.2 fusion.81
  76.3 5.5 %fusion.82 = f32[2,512,10,64]{1,3,2,0:T(8,128)} fusion(f32[2,512,10,64]{1,3,2,0:T(8,128)} %get-tuple-element.535, s32[]{:T(128)} %get-tuple-element.534, f32[512,512]{1,0:T(8,128)S(1)} %fusion.80, f32[10,512]{1,0:T(8,128)S(1)} %dynamic-slice_bitcast_fusion.3, pred[512,512]{1,0:T(8,128)(4,1)S(1)} %fusion.81, ...), kind=kOutput, calls=%fused_computation.7.clone.1.clone | convolution fusion | flops 348651520 | bytes 3343360 | tf_op jit(solution)/shard_map/while/body/eval_jaxpr/hts,shp->thp/dot_general | solution.py:115
  81.8 3.8 %multiply_reduce_fusion.3 = bf16[512,512]{1,0:T(8,128)(2,1)S(1)} fusion(f32[10,512]{1,0:T(8,128)S(1)} %dynamic-slice_bitcast_fusion.3, pred[512,512]{1,0:T(8,128)(4,1)S(1)} %fusion.81, bf16[2,512,10,64]{1,3,2,0:T(8,128)(2,1)S(1)} %copy-done.3, s32[]{:T(128)} %get-tuple-element.534, bf16[2,512,10,64]{1,3,2,0:T(8,128)(2,1)S(1)} %copy-done.2), kind=kOutput, calls=%fused_computation.1.clone.1.clone | convolution fusion | flops 348389376 | bytes 2163712 | tf_op jit(solution)/shard_map/while/body/eval_jaxpr/thp,shp->hts/dot_general | solution.py:118
  85.7 0.3 fusion.83
  86.0 0.8 copy-done.6
  86.8 1.3 add_convert_fusion.2
  88.1 0.8 copy.113
  89.1 69.2 %all-reduce.2.cloned.1.call-done = bf16[1024,128]{1,0:T(8,128)(2,1)} async-done(((bf16[1024,128]{1,0:T(8,128)(2,1)}), bf16[1024,128]{1,0:T(8,128)(2,1)}) %all-reduce.2.cloned.1.call-update) | async-done | bytes 262160 | tf_op jit(solution)/shard_map/psum | solution.py:145
  158.2 2.0 %fusion.35 = f32[128,320]{1,0:T(8,128)} fusion(bf16[1024,128]{1,0:T(8,128)(2,1)} %all-reduce.2.cloned.1.call-done, bf16[1,1024,320]{1,2,0:T(8,128)(2,1)S(1)} %copy-done), kind=kOutput, calls=%fused_computation.51 | convolution fusion | flops 83886080 | bytes 1081344 | tf_op jit(solution)/shard_map/dot_general | solution.py:147
  160.3 2.3 %add_convert_fusion = bf16[2,512,10,64]{1,3,2,0:T(8,128)(2,1)S(1)} fusion(f32[2,512,10,64]{1,3,2,0:T(8,128)} %get-tuple-element.145, bf16[2,512,128,1]{2,1,3,0:T(8,128)(2,1)S(1)} %bitcast.185, f32[2,512,10]{1,2,0:T(8,128)S(1)} %copy.108, f32[2,1,10,64,128]{4,3,2,1,0:T(8,128)S(1)} %copy-done.4, f32[2,10]{1,0:T(2,128)S(1)} %bitcast.198), kind=kOutput, calls=%fused_computation.45 | convolution fusion | flops 170065920 | bytes 4890704 | tf_op jit(solution)/shard_map/bkqn,kbhpn->bkqhp/dot_general | solution.py:97
  162.5 1.4 copy.109
  163.9 1.0 reshape.298
  164.9 1.4 copy.114
  166.3 1.7 reduce-scatter.2.cloned.1.call-done
  (53 shorter events, 0.5 us)
Async XLA Ops:
  7.2 1.1 copy-start
  7.2 55.2 %all-gather.3.cloned.1.call-start = ((), (), s32[]{:S(2)}) async-start(), calls=%async_computation.3 | async-start | bytes 2359296 | tf_op jit(solution)/shard_map/all_gather | solution.py:45
  10.3 147.9 %all-reduce.2.cloned.1.call-start = ((), (), s32[]{:S(2)}) async-start(), calls=%async_computation.1 | async-start | bytes 524288 | tf_op jit(solution)/shard_map/psum | solution.py:145
  23.0 3.7 %copy-start.1 = (bf16[1,1024,128]{2,1,0:T(8,128)(2,1)S(1)}, bf16[1,1024,128]{2,1,0:T(8,128)(2,1)}, u32[]{:S(2)}) copy-start(bf16[1,1024,128]{2,1,0:T(8,128)(2,1)} %param.14) | copy-start | bytes 786436
  65.2 5.6 %copy-start.2 = (bf16[2,512,10,64]{1,3,2,0:T(8,128)(2,1)S(1)}, bf16[2,512,10,64]{1,3,2,0:T(8,128)(2,1)}, u32[]{:S(2)}) copy-start(bf16[2,512,10,64]{1,3,2,0:T(8,128)(2,1)} %get-tuple-element.546) | copy-start | bytes 3932164 | tf_op jit(solution)/shard_map/while
  65.2 5.5 %copy-start.3 = (bf16[2,512,10,64]{1,3,2,0:T(8,128)(2,1)S(1)}, bf16[2,512,10,64]{1,3,2,0:T(8,128)(2,1)}, u32[]{:S(2)}) copy-start(bf16[2,512,10,64]{1,3,2,0:T(8,128)(2,1)} %get-tuple-element.551) | copy-start | bytes 3932164 | tf_op jit(solution)/shard_map/while
  70.7 3.9 %copy-start.5 = (f32[2,512,128]{1,2,0:T(8,128)S(1)}, f32[2,512,128]{1,2,0:T(8,128)}, u32[]{:S(2)}) copy-start(f32[2,512,128]{1,2,0:T(8,128)} %get-tuple-element.536) | copy-start | bytes 1572868 | tf_op jit(solution)/shard_map/while
  74.9 0.8 copy-start.6
  76.2 5.6 %copy-start.2 = (bf16[2,512,10,64]{1,3,2,0:T(8,128)(2,1)S(1)}, bf16[2,512,10,64]{1,3,2,0:T(8,128)(2,1)}, u32[]{:S(2)}) copy-start(bf16[2,512,10,64]{1,3,2,0:T(8,128)(2,1)} %get-tuple-element.546) | copy-start | bytes 3932164 | tf_op jit(solution)/shard_map/while
  76.3 5.6 %copy-start.3 = (bf16[2,512,10,64]{1,3,2,0:T(8,128)(2,1)S(1)}, bf16[2,512,10,64]{1,3,2,0:T(8,128)(2,1)}, u32[]{:S(2)}) copy-start(bf16[2,512,10,64]{1,3,2,0:T(8,128)(2,1)} %get-tuple-element.551) | copy-start | bytes 3932164 | tf_op jit(solution)/shard_map/while
  81.8 3.9 %copy-start.5 = (f32[2,512,128]{1,2,0:T(8,128)S(1)}, f32[2,512,128]{1,2,0:T(8,128)}, u32[]{:S(2)}) copy-start(f32[2,512,128]{1,2,0:T(8,128)} %get-tuple-element.536) | copy-start | bytes 1572868 | tf_op jit(solution)/shard_map/while
  86.0 0.8 copy-start.6
  86.8 73.4 %copy-start.4 = (f32[2,1,10,64,128]{4,3,2,1,0:T(8,128)S(1)}, f32[2,1,10,64,128]{4,3,2,1,0:T(8,128)}, u32[]{:S(2)}) copy-start(f32[2,1,10,64,128]{4,3,2,1,0:T(8,128)} %get-tuple-element.146) | copy-start | bytes 1966084
  89.0 79.0 %reduce-scatter.2.cloned.1.call-start = ((), (), s32[]{:S(2)}) async-start(), calls=%async_computation.2 | async-start | bytes 294912 | tf_op jit(solution)/shard_map/reduce_scatter | solution.py:146
Sparse Core Ops, SparseCore 0:
  10.4 51.9 all-gather.2
  89.1 69.0 all-reduce.1
  161.1 6.8 reduce-scatter.1
